TPU v7x, 512 devices: a whole 4x8x8 slice. The times are simulated.
512 devices in a mesh: clip: 32 (over z, x_lo, core), sp: 16 (over y, x_hi).
Axes of the slice: x: 4 (x_hi: 2, x_lo: 2; x = x_hi * 2 + x_lo), y: 8, z: 8, core: 2. Of those that a mesh axis runs over, the one named last changes fastest.
Arguments:
- features: bfloat16 [2, 3, 32, 4, 128, 2048], P(None, None, 'clip', None, 'sp'), may hold values from -6 to 6, as said below
- context: bfloat16 [32, 2, 64, 2048], P('clip', None, None, 'sp'), may hold values from -6 to 6
- scene_cuts: int32 [32], replicated, may hold values 0 or 1
- key_clips: int32 [4], replicated, may hold values from 0 to 31, as said below
- owner_slot: int32 [32, 2], P('clip'), may hold values from 0 to 3
Outputs:
- mixed: bfloat16 [2, 32, 4, 128, 2048], P(None, 'clip', None, 'sp')
Inputs may be any that keep to these rules, and one draw needn't show every extreme that they name: `features`: keys and values lie within the range; queries too. `key_clips`: 4 distinct clips; clip 0 and clip 32 - 1 are always among them.
All inputs are finite; a program needn't handle non-finite values.
Results may differ from a plain program's by a relative error of at most 0.0042.
Values may be sent and summed in bfloat16 or wider, within the bound.
A program may use at most 64 MiB of HBM per device.

v0:
```python
import jax
import jax.numpy as jnp
from jax import lax
from jax.sharding import PartitionSpec as P

HEAD_DIM = 64
POOL = 2


NEG_FILL = -1e30


def padded_2(cells, sides, width):
    for axis, dim in sides:
        count = lax.axis_size(axis)
        ends = count - 1
        head = lax.slice_in_dim(cells, 0, width, axis=dim)
        tail = lax.slice_in_dim(cells, cells.shape[dim] - width, cells.shape[dim], axis=dim)
        cells = jnp.concatenate(
            [
                lax.ppermute(tail, axis, [(i, (i + 1) % count) for i in range(ends)]),
                cells,
                lax.ppermute(head, axis, [((i + 1) % count, i) for i in range(ends)]),
            ],
            axis=dim,
        )
    return cells


def shortened(x):

    def short(part):
        return part.astype(jnp.bfloat16) if part.dtype == jnp.float32 else part

    return jax.tree.map(short, x)


def attend_block(queries, key_heads, value_heads, usable, head_width):
    pieces = []
    for head_pos in range(len(key_heads)):
        lower = head_pos * head_width
        query_head = queries[:, lower : lower + head_width]
        scores = jnp.einsum(
            "qe,ke->qk", query_head, key_heads[head_pos], preferred_element_type=jnp.float32
        ) * head_width ** (-0.5)
        scores = jnp.where(usable[None, :], scores, NEG_FILL)
        top_score = jnp.max(scores, axis=1, keepdims=True)
        weights = jnp.exp(scores - top_score)
        total = jnp.sum(weights, axis=1, keepdims=True)
        rounded = weights.astype(jnp.bfloat16)
        summed = jnp.dot(rounded, value_heads[head_pos], preferred_element_type=jnp.float32)
        pieces.append((summed / total).astype(jnp.bfloat16))
    return jnp.concatenate(pieces, axis=1)


def attend_all(queries, all_keys, all_values, usable):
    head_width = HEAD_DIM
    head_count = queries.shape[1] // head_width
    key_heads = [
        all_keys[:, pos * head_width : (pos + 1) * head_width] for pos in range(head_count)
    ]
    value_heads = [
        all_values[:, pos * head_width : (pos + 1) * head_width] for pos in range(head_count)
    ]
    row_count = queries.shape[0]
    block_rows = 512

    def one_block(offset):
        return attend_block(queries, key_heads, value_heads, usable, head_width)

    offsets = jnp.arange(row_count // block_rows, dtype=jnp.int32) * block_rows
    return lax.map(one_block, offsets).reshape(row_count, queries.shape[1])


def on_device(features, context, scene_cuts, key_clips, owner_slot):
    clip_index = lax.axis_index("clip")
    clip_count = lax.axis_size("clip")
    frame_count = features.shape[3]
    before_ok = (clip_index > 0) & (scene_cuts[clip_index] == 0)
    after_ok = (clip_index < clip_count - 1) & (
        scene_cuts[jnp.minimum(clip_index + 1, clip_count - 1)] == 0
    )
    owners = key_clips[owner_slot[0]]

    def regroup(step_index):
        return lax.all_to_all(features[step_index], "sp", split_axis=4, concat_axis=3, tiled=True)

    grouped = regroup(0)
    padded = padded_2(grouped[1:3, 0], (("clip", 1),), 1)
    edges = jnp.stack([padded[:, 0], padded[:, frame_count + 1]], axis=1)

    def fetch(local_context):
        gathered = lax.all_gather(local_context[None], "clip", axis=0, tiled=True)
        return gathered[owners]

    def attend_step(group, chosen):
        spatial = group.shape[3]
        lane_count = group.shape[4]
        queries = group[0, 0].reshape(-1, lane_count)
        all_keys = jnp.concatenate(
            [
                group[1, 0].reshape(-1, lane_count),
                edges[0, 0],
                edges[0, 1],
                chosen[:, 0].reshape(-1, lane_count),
            ]
        )
        all_values = jnp.concatenate(
            [
                group[2, 0].reshape(-1, lane_count),
                edges[1, 0],
                edges[1, 1],
                chosen[:, 1].reshape(-1, lane_count),
            ]
        )
        usable = jnp.concatenate(
            [
                jnp.ones((queries.shape[0],), jnp.bool_),
                jnp.broadcast_to(before_ok, (spatial,)),
                jnp.broadcast_to(after_ok, (spatial,)),
                jnp.ones((chosen.shape[0] * chosen.shape[2],), jnp.bool_),
            ]
        )
        attended = attend_all(queries, all_keys, all_values, usable).reshape(
            1, frame_count, spatial, lane_count
        )
        return lax.all_to_all(
            shortened(attended), "sp", split_axis=2, concat_axis=3, tiled=True
        ).astype(attended.dtype)

    result_first = attend_step(grouped, fetch(context[0]))
    regrouped = regroup(1)
    lane_total = grouped.shape[4]
    first_frame = grouped[1:3, 0, 0].astype(jnp.float32)
    pooled = (first_frame.reshape(2, -1, POOL, lane_total).sum(axis=2) * POOL ** (-0.5)).astype(
        jnp.bfloat16
    )
    result_second = attend_step(regrouped, fetch(pooled))
    return jnp.stack([result_first, result_second])


def solution(mesh):
    placed = (
        P(None, None, "clip", None, "sp", None),
        P("clip", None, None, "sp"),
        P(),
        P(),
        P("clip", None),
    )
    return jax.shard_map(
        on_device,
        mesh=mesh,
        in_specs=placed,
        out_specs=P(None, "clip", None, "sp", None),
        check_vma=False,
    )
```

profile of v0, /device:TPU:1, one launch (start us, length us, event | category | flops | bytes accessed | tf_op | source)
XLA Modules:
  0.0 224.2 jit_solution(11979157746685587107)
XLA Ops:
  8.4 7.0 %copy.41 = bf16[1,3,1,4,8,2048]{4,3,1,5,2,0:T(4,128)(2,1)} copy(bf16[1,3,1,4,8,2048]{5,4,3,2,1,0:T(8,128)(2,1)S(1)} %get-tuple-element.51) | data formatting | bytes 786432
  15.4 7.7 %bitcast_bitcast_fusion.1 = bf16[2048,1,3,4,8]{4,3,2,1,0:T(4,128)(2,1)} fusion(bf16[1,3,1,4,8,2048]{4,3,1,5,2,0:T(4,128)(2,1)} %copy.41), kind=kLoop, calls=%fused_computation.106 | loop fusion | bytes 786432
  23.1 14.5 %reshape.115 = bf16[16,2,6144]{2,1,0:T(2,128)(2,1)} reshape(bf16[2048,1,3,4,8]{4,3,2,1,0:T(4,128)(2,1)} %bitcast_bitcast_fusion.1) | data formatting | bytes 786432
  37.5 10.2 %all-to-all-start = ((bf16[16,2,6144]{2,1,0:T(2,128)(2,1)}), bf16[16,2,6144]{2,1,0:T(2,128)(2,1)S(1)}, u32[]{:S(2)}, u32[]{:S(2)}) async-start(bf16[16,2,6144]{2,1,0:T(2,128)(2,1)} %reshape.115), calls=%async_computation | async-start | bytes 786432 | tf_op jit(solution)/shard_map/all_to_all | solution.py:86
  47.8 7.0 %copy.42 = bf16[1,3,1,4,8,2048]{4,3,1,5,2,0:T(4,128)(2,1)} copy(bf16[1,3,1,4,8,2048]{5,4,3,2,1,0:T(8,128)(2,1)S(1)} %get-tuple-element.50) | data formatting | bytes 786432
  54.7 7.7 %bitcast_bitcast_fusion = bf16[2048,1,3,4,8]{4,3,2,1,0:T(4,128)(2,1)} fusion(bf16[1,3,1,4,8,2048]{4,3,1,5,2,0:T(4,128)(2,1)} %copy.42), kind=kLoop, calls=%fused_computation.105 | loop fusion | bytes 786432
  62.4 14.5 %reshape.117 = bf16[16,2,6144]{2,1,0:T(2,128)(2,1)} reshape(bf16[2048,1,3,4,8]{4,3,2,1,0:T(4,128)(2,1)} %bitcast_bitcast_fusion) | data formatting | bytes 786432
  76.9 9.1 %all-to-all-start.2 = ((bf16[16,2,6144]{2,1,0:T(2,128)(2,1)}), bf16[16,2,6144]{2,1,0:T(2,128)(2,1)S(1)}, u32[]{:S(2)}, u32[]{:S(2)}) async-start(bf16[16,2,6144]{2,1,0:T(2,128)(2,1)} %reshape.117), calls=%async_computation.2 | async-start | bytes 786432 | tf_op jit(solution)/shard_map/all_to_all | solution.py:86
  86.2 8.4 %reshape.116 = bf16[2048,1,3,4,8]{4,3,2,1,0:T(4,128)(2,1)} reshape(bf16[16,2,6144]{2,1,0:T(2,128)(2,1)S(1)} %all-to-all-done) | data formatting | bytes 786432
  94.5 8.2 %copy.40 = bf16[3,1,4,8,16,128]{5,3,4,2,0,1:T(8,128)(2,1)S(1)} copy(bf16[3,1,4,8,16,128]{3,2,0,5,4,1:T(4,128)(2,1)} %bitcast.69) | data formatting | bytes 786432 | tf_op jit(solution)/shard_map/all_to_all | solution.py:86
  106.2 6.5 %copy.38 = bf16[3,1,4,8,16,128]{5,4,3,2,0,1:T(8,128)(2,1)S(1)} copy(bf16[3,1,4,8,16,128]{3,2,0,5,4,1:T(4,128)(2,1)} %bitcast.70) | data formatting | bytes 786432 | tf_op jit(solution)/shard_map/all_to_all | solution.py:86
  112.7 8.4 %reshape.118 = bf16[2048,1,3,4,8]{4,3,2,1,0:T(4,128)(2,1)} reshape(bf16[16,2,6144]{2,1,0:T(2,128)(2,1)S(1)} %all-to-all-done.2) | data formatting | bytes 786432
  121.1 6.5 %copy.39 = bf16[3,1,4,8,16,128]{5,4,3,2,0,1:T(8,128)(2,1)S(1)} copy(bf16[3,1,4,8,16,128]{3,2,0,5,4,1:T(4,128)(2,1)} %bitcast.71) | data formatting | bytes 786432 | tf_op jit(solution)/shard_map/all_to_all | solution.py:86
  127.6 3.6 %collective-permute-start = (bf16[2,1,128,128]{3,2,1,0:T(8,128)(2,1)S(1)}, bf16[2,1,128,128]{3,2,1,0:T(8,128)(2,1)S(1)}, u32[]{:S(2)}, u32[]{:S(2)}) collective-permute-start(bf16[2,1,128,128]{3,2,1,0:T(8,128)(2,1)S(1)} %get-tuple-element.68), channel_id=1, source_target_pairs={{0,16},{16,32},{32,48},{48,64},{64,80},{80,96},{96,112},{112,128},... | collective-permute-start | bytes 196616 | tf_op jit(solution)/shard_map/ppermute | solution.py:21
  131.5 1.9 collective-permute-start.1
  133.5 3.9 %collective-permute-done.1 = bf16[2,1,128,128]{3,2,1,0:T(8,128)(2,1)S(1)} collective-permute-done((bf16[2,1,128,128]{3,2,1,0:T(8,128)(2,1)S(1)}, bf16[2,1,128,128]{3,2,1,0:T(8,128)(2,1)S(1)}, u32[]{:S(2)}, u32[]{:S(2)}) %collective-permute-start.1) | collective-permute-done | bytes 65568 | tf_op jit(solution)/shard_map/ppermute | solution.py:23
  137.5 1.8 gather_fusion.1
  139.3 37.1 %all-gather.6.cloned.1.call-done = bf16[64,64,128]{2,1,0:T(8,128)(2,1)} async-done(((bf16[2,64,128]{2,1,0:T(8,128)(2,1)}), bf16[64,64,128]{2,1,0:T(8,128)(2,1)}) %all-gather.6.cloned.1.call-update) | async-done | bytes 1048592 | tf_op jit(solution)/shard_map/all_gather | solution.py:93
  176.4 1.8 gather_fusion.2
  179.6 1.3 fusion.4
  184.2 8.7 %all-to-all-start.3 = ((bf16[1,4,128,128]{3,1,0,2:T(4,128)(2,1)}), bf16[1,4,128,128]{3,1,0,2:T(4,128)(2,1)S(1)}, u32[]{:S(2)}, u32[]{:S(2)}) async-start(bf16[1,4,128,128]{3,1,0,2:T(4,128)(2,1)} %copy.36), calls=%async_computation.3 | async-start | bytes 262144 | tf_op jit(solution)/shard_map/all_to_all | solution.py:127
  195.9 7.1 %all-to-all-done.3 = bf16[1,4,128,128]{3,1,0,2:T(4,128)(2,1)S(1)} async-done(((bf16[1,4,128,128]{3,1,0,2:T(4,128)(2,1)}), bf16[1,4,128,128]{3,1,0,2:T(4,128)(2,1)S(1)}, u32[]{:S(2)}, u32[]{:S(2)}) %all-to-all-start.3) | async-done | bytes 131104 | tf_op jit(solution)/shard_map/all_to_all | solution.py:127
  203.1 3.5 %all-to-all-start.1 = ((bf16[1,4,128,128]{3,1,0,2:T(4,128)(2,1)}), bf16[1,4,128,128]{3,1,0,2:T(4,128)(2,1)S(1)}, u32[]{:S(2)}, u32[]{:S(2)}) async-start(bf16[1,4,128,128]{3,1,0,2:T(4,128)(2,1)} %copy.28), calls=%async_computation.1 | async-start | bytes 262144 | tf_op jit(solution)/shard_map/all_to_all | solution.py:127
  206.6 10.0 %all-to-all-done.1 = bf16[1,4,128,128]{3,1,0,2:T(4,128)(2,1)S(1)} async-done(((bf16[1,4,128,128]{3,1,0,2:T(4,128)(2,1)}), bf16[1,4,128,128]{3,1,0,2:T(4,128)(2,1)S(1)}, u32[]{:S(2)}, u32[]{:S(2)}) %all-to-all-start.1) | async-done | bytes 131104 | tf_op jit(solution)/shard_map/all_to_all | solution.py:127
  (66 shorter events, 13.1 us)
Async XLA Ops:
  6.5 99.0 %copy-start = (s32[4]{0:T(128)S(1)}, s32[4]{0:T(128)}, u32[]{:S(2)}) copy-start(s32[4]{0:T(128)} %param.8) | copy-start | bytes 52
  6.5 130.9 %all-gather.4.cloned.1.call-start = ((), (), s32[]{:S(2)}) async-start(), calls=%async_computation.4 | async-start | bytes 1081344 | tf_op jit(solution)/shard_map/all_gather | solution.py:93
  37.5 39.3 %all-to-all-start = ((bf16[16,2,6144]{2,1,0:T(2,128)(2,1)}), bf16[16,2,6144]{2,1,0:T(2,128)(2,1)S(1)}, u32[]{:S(2)}, u32[]{:S(2)}) async-start(bf16[16,2,6144]{2,1,0:T(2,128)(2,1)} %reshape.115), calls=%async_computation | async-start | bytes 786432 | tf_op jit(solution)/shard_map/all_to_all | solution.py:86
  76.9 35.8 %all-to-all-start.2 = ((bf16[16,2,6144]{2,1,0:T(2,128)(2,1)}), bf16[16,2,6144]{2,1,0:T(2,128)(2,1)S(1)}, u32[]{:S(2)}, u32[]{:S(2)}) async-start(bf16[16,2,6144]{2,1,0:T(2,128)(2,1)} %reshape.117), calls=%async_computation.2 | async-start | bytes 786432 | tf_op jit(solution)/shard_map/all_to_all | solution.py:86
  85.9 90.4 %all-gather.6.cloned.1.call-start = ((), (), s32[]{:S(2)}) async-start(), calls=%async_computation.5 | async-start | bytes 1081344 | tf_op jit(solution)/shard_map/all_gather | solution.py:93
  94.5 9.1 %copy-start.4 = (s32[1,2]{1,0:T(1,128)S(1)}, s32[1,2]{1,0:T(1,128)}, u32[]{:S(2)}) copy-start(s32[1,2]{1,0:T(1,128)} %param.9) | copy-start | bytes 28
  94.5 9.1 %copy-start.3 = (s32[32]{0:T(128)S(1)}, s32[32]{0:T(128)}, u32[]{:S(2)}) copy-start(s32[32]{0:T(128)} %param.7) | copy-start | bytes 388
  127.6 5.9 %collective-permute-start = (bf16[2,1,128,128]{3,2,1,0:T(8,128)(2,1)S(1)}, bf16[2,1,128,128]{3,2,1,0:T(8,128)(2,1)S(1)}, u32[]{:S(2)}, u32[]{:S(2)}) collective-permute-start(bf16[2,1,128,128]{3,2,1,0:T(8,128)(2,1)S(1)} %get-tuple-element.68), channel_id=1, source_target_pairs={{0,16},{16,32},{32,48},{48,64},{64,80},{80,96},{96,112},{112,128},... | collective-permute-start | bytes 196616 | tf_op jit(solution)/shard_map/ppermute | solution.py:21
  131.5 5.9 %collective-permute-start.1 = (bf16[2,1,128,128]{3,2,1,0:T(8,128)(2,1)S(1)}, bf16[2,1,128,128]{3,2,1,0:T(8,128)(2,1)S(1)}, u32[]{:S(2)}, u32[]{:S(2)}) collective-permute-start(bf16[2,1,128,128]{3,2,1,0:T(8,128)(2,1)S(1)} %get-tuple-element.69), channel_id=1, source_target_pairs={{16,0},{32,16},{48,32},{64,48},{80,64},{96,80},{112,96},{128,112},... | collective-permute-start | bytes 196616 | tf_op jit(solution)/shard_map/ppermute | solution.py:23
  180.9 1.2 copy-start.1
  184.2 18.8 %all-to-all-start.3 = ((bf16[1,4,128,128]{3,1,0,2:T(4,128)(2,1)}), bf16[1,4,128,128]{3,1,0,2:T(4,128)(2,1)S(1)}, u32[]{:S(2)}, u32[]{:S(2)}) async-start(bf16[1,4,128,128]{3,1,0,2:T(4,128)(2,1)} %copy.36), calls=%async_computation.3 | async-start | bytes 262144 | tf_op jit(solution)/shard_map/all_to_all | solution.py:127
  192.9 1.5 copy-start.2
  203.1 13.6 %all-to-all-start.1 = ((bf16[1,4,128,128]{3,1,0,2:T(4,128)(2,1)}), bf16[1,4,128,128]{3,1,0,2:T(4,128)(2,1)S(1)}, u32[]{:S(2)}, u32[]{:S(2)}) async-start(bf16[1,4,128,128]{3,1,0,2:T(4,128)(2,1)} %copy.28), calls=%async_computation.1 | async-start | bytes 262144 | tf_op jit(solution)/shard_map/all_to_all | solution.py:127
Sparse Core Ops, SparseCore 0:
  9.5 72.6 all-gather.3
  103.7 72.5 all-gather.5
where the time goes:
time: 226 us; the launch traced here: 224 us
  local copies, waits for them, and re-layouts  105 us (46%)
  waiting for transfers between devices  58.9 us (26%)
  starting transfers between devices  37.2 us (16%)
  between operations  15 us (7%)
  matrix products  5.1 us (2%)
  other arithmetic  2.84 us (1%)
    unnamed x18, local copies, waits for them, and re-layouts  75.9 us
    all_gather x2, waiting for transfers between devices, fetch(): gathered = lax.all_gather(local_context[None], 'clip', axis=0, tiled=True)  37.1 us
    all_to_all x3, local copies, waits for them, and re-layouts, regroup(): lax.all_to_all(features[step_index], 'sp', split_axis=4, concat_axis=3, t...  21.1 us
    all_to_all x2, starting transfers between devices, regroup(): lax.all_to_all(features[step_index], 'sp', split_axis=4, concat_axis=3, t...  19.3 us
    all_to_all x2, waiting for transfers between devices, attend_step(): lax.all_to_all(shortened(attended), 'sp', split_axis=2, concat_axis=3, ti...  17.1 us
    all_to_all x2, starting transfers between devices, attend_step(): lax.all_to_all(shortened(attended), 'sp', split_axis=2, concat_axis=3, ti...  12.2 us
  transfers between devices with their start and end apart: 8, of which 4 were waited for; matrix products, arithmetic and copies ran while one was open for 46% of the time, Pallas kernels for 0%

commit v1 on v0

v1 whole, which is shorter than its diff:
```python
import functools

import jax
import jax.numpy as jnp
from jax import lax
from jax.experimental import pallas as pl
from jax.experimental.pallas import tpu as pltpu
from jax.sharding import PartitionSpec as P

HEAD_DIM = 64
LANES = 128
QUAD = 4
MESH = pl.DeviceIdType.MESH


def wait_bytes(ref, sem):
    pltpu.make_async_copy(ref, ref, sem).wait()


def flat(block):
    wide = block.astype(jnp.float32)
    return wide.reshape(-1, LANES).astype(jnp.bfloat16)


def kernel(
    clips,
    sps,
    feat,
    ctx,
    cuts,
    key_clips,
    slots,
    out,
    recv,
    edge,
    pooled,
    scat_0,
    scat_1,
    pick,
    quad_0,
    quad_1,
    full_0,
    full_1,
    keys,
    vals,
    done,
    in_send,
    in_recv,
    own_sem,
    edge_send,
    edge_recv,
    ex_send,
    ex_recv,
    out_send,
    out_recv,
):
    c = lax.axis_index("clip")
    s = lax.axis_index("sp")
    zs = clips // QUAD
    z = c // QUAD
    q = c % QUAD
    frames = recv.shape[2]
    tiles = ctx.shape[0]
    part = tiles // zs
    frame_rows = sps * 8
    own_rows = frames * frame_rows
    ctx_rows = tiles * 4
    scat, quad, full = (scat_0, scat_1), (quad_0, quad_1), (full_0, full_1)

    barrier = pltpu.get_barrier_semaphore()

    def greet(clip, sp):
        pl.semaphore_signal(barrier, inc=1, device_id=(clip, sp), device_id_type=MESH)

    def greet_sp(k, _):
        greet(c, (s + k) % sps)
        return 0

    def greet_z(k, _):
        greet(((z + k) % zs) * QUAD + q, s)
        return 0

    def greet_quad(k, _):
        greet(z * QUAD + (q + k) % QUAD, s)
        return 0

    before = (c + clips - 1) % clips
    after = (c + 1) % clips
    lax.fori_loop(1, sps, greet_sp, 0)
    lax.fori_loop(1, zs, greet_z, 0)
    lax.fori_loop(1, QUAD, greet_quad, 0)
    greet(before, s)
    greet(after, s)
    pl.semaphore_wait(barrier, sps - 1 + zs - 1 + QUAD - 1 + 2)

    def remote(src, dst, send, rcv, clip, sp):
        pltpu.make_async_remote_copy(
            src_ref=src,
            dst_ref=dst,
            send_sem=send,
            recv_sem=rcv,
            device_id=(clip, sp),
            device_id_type=MESH,
        ).start()

    groups = ((0, 1, 2), (0, 0, 1), (1, 0, 3))

    def block(ref, group, sp):
        step, low, size = group
        return ref.at[step, pl.ds(low, size), :, :, pl.ds(sp * LANES, LANES)]

    def place(group, sp):
        step, low, size = group
        return recv.at[step, pl.ds(low, size), :, sp]

    def send_group(g):
        group = groups[g]

        def one(k, _):
            to = (s + k) % sps
            remote(block(feat, group, to), place(group, s), in_send.at[g], in_recv.at[g], c, to)
            return 0

        pltpu.make_async_copy(block(feat, group, s), place(group, s), own_sem.at[g]).start()
        lax.fori_loop(1, sps, one, 0)

    def others(group):
        step, low, size = group
        return recv.at[step, pl.ds(low, size), :, pl.ds(0, sps - 1)]

    def wait_group(g):
        pltpu.make_async_copy(block(feat, groups[g], s), place(groups[g], s), own_sem.at[g]).wait()
        wait_bytes(others(groups[g]), in_recv.at[g])

    def scatter(e, src):
        def one(k, _):
            to = (z + k) % zs
            remote(
                src.at[pl.ds(to * part, part)],
                scat[e].at[z],
                ex_send.at[e, 0],
                ex_recv.at[e, 0],
                to * QUAD + q,
                s,
            )
            return 0

        lax.fori_loop(1, zs, one, 0)
        own = pltpu.make_async_copy(src.at[pl.ds(z * part, part)], scat[e].at[z], own_sem.at[3 + e])
        own.start()
        own.wait()

    def exchange(e):
        wait_bytes(scat[e].at[pl.ds(0, zs - 1)], ex_recv.at[e, 0])
        for i in range(QUAD):
            pick[e, i] = scat[e][key_clips[i] // QUAD]

        def one(k, _):
            remote(
                pick.at[e],
                quad[e].at[q],
                ex_send.at[e, 1],
                ex_recv.at[e, 1],
                z * QUAD + (q + k) % QUAD,
                s,
            )
            return 0

        lax.fori_loop(1, QUAD, one, 0)
        quad[e][q] = pick[e]

    def gather(e):
        wait_bytes(quad[e].at[pl.ds(0, QUAD - 1)], ex_recv.at[e, 1])
        for i in range(QUAD):
            full[e][z, i] = quad[e][key_clips[i] % QUAD, i]

        def one(k, _):
            remote(
                full[e].at[z],
                full[e].at[z],
                ex_send.at[e, 2],
                ex_recv.at[e, 2],
                ((z + k) % zs) * QUAD + q,
                s,
            )
            return 0

        lax.fori_loop(1, zs, one, 0)

    scatter(0, ctx)
    send_group(0)
    send_group(1)
    send_group(2)
    exchange(0)
    gather(0)

    wait_group(0)
    remote(recv.at[0, pl.ds(1, 2), frames - 1], edge.at[0], edge_send.at[0], edge_recv.at[0], after, s)
    remote(recv.at[0, pl.ds(1, 2), 0], edge.at[1], edge_send.at[1], edge_recv.at[1], before, s)
    half = tiles // 2
    row = lax.broadcasted_iota(jnp.int32, (half * 8, frame_rows), 0)
    col = lax.broadcasted_iota(jnp.int32, (half * 8, frame_rows), 1)
    pairs = ((col == 2 * row) | (col == 2 * row + 1)).astype(jnp.bfloat16)
    for j in range(2):
        added = jnp.dot(pairs, flat(recv[0, 1 + j, 0]), preferred_element_type=jnp.float32)
        pooled[pl.ds(j * half, half)] = (added * 2**-0.5).reshape(half, 8, LANES).astype(jnp.bfloat16)
    scatter(1, pooled)

    before_ok = (c > 0) & (cuts[c] == 0)
    after_ok = (c < clips - 1) & (cuts[after] == 0)
    lane = lax.broadcasted_iota(jnp.int32, (1, LANES), 1)
    first = lane < HEAD_DIM

    def put(step, base, key_rows, value_rows, ok=None):
        rows = key_rows.shape[0]
        where = pl.ds(base, rows)
        ones = jnp.ones((rows, LANES), jnp.float32)
        value_rows = value_rows.astype(jnp.float32)
        if ok is not None:
            value_rows = jnp.where(ok, value_rows, 0.0)
            ones = jnp.where(ok, ones, 0.0)
        keys[step, where] = key_rows
        vals[step, 0, where] = jnp.where(first, value_rows, ones).astype(jnp.bfloat16)
        vals[step, 1, where] = jnp.where(first, ones, value_rows).astype(jnp.bfloat16)

    def put_own(step):
        for f in range(frames):
            put(step, f * frame_rows, flat(recv[step, 1, f]), flat(recv[step, 2, f]))

    def put_edge(step):
        for side, ok in ((0, before_ok), (1, after_ok)):
            own = recv[step, 1, 0].astype(jnp.float32)
            key_rows = jnp.where(ok, edge[side, 0].astype(jnp.float32), own)
            key_rows = key_rows.reshape(-1, LANES).astype(jnp.bfloat16)
            put(step, own_rows + side * frame_rows, key_rows, flat(edge[side, 1]), ok)

    def put_context(step):
        wait_bytes(full[step].at[pl.ds(0, zs - 1)], ex_recv.at[step, 2])
        for i in range(2):
            base = own_rows + 2 * frame_rows + i * ctx_rows
            taken = flat(full[step][:, slots[i]])
            put(step, base, taken[:ctx_rows], taken[ctx_rows:])

    def attend(step, f):
        queries = flat(recv[step, 0, f]).astype(jnp.float32) * HEAD_DIM**-0.5
        both = jnp.concatenate(
            [jnp.where(first, queries, 0.0), jnp.where(first, 0.0, queries)], axis=0
        ).astype(jnp.bfloat16)
        scores = lax.dot_general(
            both, keys[step], (((1,), (1,)), ((), ())), preferred_element_type=jnp.float32
        )
        top = jnp.max(scores, axis=1, keepdims=True)
        weights = jnp.exp(scores - top).astype(jnp.bfloat16)
        left = jnp.dot(weights[:frame_rows], vals[step, 0], preferred_element_type=jnp.float32)
        right = jnp.dot(weights[frame_rows:], vals[step, 1], preferred_element_type=jnp.float32)
        numer = jnp.where(first, left, right)
        total = pltpu.roll(jnp.where(first, right, left), HEAD_DIM, 1)
        done[step, f] = (numer / total).reshape(sps, 8, LANES).astype(jnp.bfloat16)

    def send_out(step):
        def one(k, _):
            to = (s + k) % sps
            remote(
                done.at[step, :, to],
                out.at[step, :, :, pl.ds(s * LANES, LANES)],
                out_send.at[step],
                out_recv.at[step],
                c,
                to,
            )
            return 0

        lax.fori_loop(1, sps, one, 0)
        pltpu.make_async_copy(
            done.at[step, :, s], out.at[step, :, :, pl.ds(s * LANES, LANES)], own_sem.at[5 + step]
        ).start()

    put_own(0)
    exchange(1)
    wait_group(1)
    wait_bytes(edge.at[0], edge_recv.at[0])
    wait_bytes(edge.at[1], edge_recv.at[1])
    put_edge(0)
    put_context(0)
    for f in range(frames):
        attend(0, f)
        if f == 0:
            gather(1)
    send_out(0)

    wait_group(2)
    put_own(1)
    put_edge(1)
    put_context(1)
    for f in range(frames):
        attend(1, f)
    send_out(1)

    for g in range(3):
        wait_bytes(others(groups[g]), in_send.at[g])
    for side in range(2):
        wait_bytes(edge.at[side], edge_send.at[side])
    for e in range(2):
        wait_bytes(scat[e].at[pl.ds(0, zs - 1)], ex_send.at[e, 0])
        wait_bytes(quad[e].at[pl.ds(0, QUAD - 1)], ex_send.at[e, 1])
        wait_bytes(full[e].at[pl.ds(0, zs - 1)], ex_send.at[e, 2])
    for step in range(2):
        wait_bytes(done.at[step, :, pl.ds(0, sps - 1)], out_send.at[step])
        wait_bytes(done.at[step, :, pl.ds(0, sps - 1)], out_recv.at[step])
        pltpu.make_async_copy(
            done.at[step, :, s], out.at[step, :, :, pl.ds(s * LANES, LANES)], own_sem.at[5 + step]
        ).wait()


def on_device(clips, sps, features, context, scene_cuts, key_clips, owner_slot):
    steps, kinds, _, frames, tokens, width = features.shape
    tiles = context.shape[1] * context.shape[2] // 8
    part = tiles // (clips // QUAD)
    zs = clips // QUAD
    key_rows = frames * sps * 8 + 2 * sps * 8 + tiles * 8
    dma = pltpu.SemaphoreType.DMA
    half = jnp.bfloat16
    smem = pl.BlockSpec(memory_space=pltpu.SMEM)
    anywhere = pl.BlockSpec(memory_space=pl.ANY)
    mixed = pl.pallas_call(
        functools.partial(kernel, clips, sps),
        out_shape=jax.ShapeDtypeStruct((steps, frames, tokens, width), half),
        in_specs=[anywhere, anywhere, smem, smem, smem],
        out_specs=anywhere,
        scratch_shapes=[
            pltpu.VMEM((steps, kinds, frames, sps, 8, LANES), half),
            pltpu.VMEM((2, 2, sps, 8, LANES), half),
            pltpu.VMEM((tiles, 8, LANES), half),
            pltpu.VMEM((zs, part, 8, LANES), half),
            pltpu.VMEM((zs, part, 8, LANES), half),
            pltpu.VMEM((2, QUAD, part, 8, LANES), half),
            pltpu.VMEM((QUAD, QUAD, part, 8, LANES), half),
            pltpu.VMEM((QUAD, QUAD, part, 8, LANES), half),
            pltpu.VMEM((zs, QUAD, part, 8, LANES), half),
            pltpu.VMEM((zs, QUAD, part, 8, LANES), half),
            pltpu.VMEM((2, key_rows, LANES), half),
            pltpu.VMEM((2, 2, key_rows, LANES), half),
            pltpu.VMEM((steps, frames, sps, 8, LANES), half),
            dma((3,)),
            dma((3,)),
            dma((7,)),
            dma((2,)),
            dma((2,)),
            dma((2, 3)),
            dma((2, 3)),
            dma((2,)),
            dma((2,)),
        ],
        compiler_params=pltpu.CompilerParams(
            collective_id=0, has_side_effects=True, vmem_limit_bytes=40 * 2**20
        ),
    )(
        features.reshape(steps, kinds, frames, tokens, width),
        context.reshape(tiles, 8, LANES),
        scene_cuts,
        key_clips,
        owner_slot.reshape(-1),
    )
    return mixed.reshape(steps, 1, frames, tokens, width)


def solution(mesh):
    placed = (
        P(None, None, "clip", None, "sp", None),
        P("clip", None, None, "sp"),
        P(),
        P(),
        P("clip", None),
    )
    return jax.shard_map(
        functools.partial(on_device, mesh.shape["clip"], mesh.shape["sp"]),
        mesh=mesh,
        in_specs=placed,
        out_specs=P(None, "clip", None, "sp", None),
        check_vma=False,
    )
```

time: 226 us -> 53.6 us (0.24)
  local copies, waits for them, and re-layouts: 105 us -> 3.28 us
  waiting for transfers between devices: 58.9 us -> 0 us
  Pallas kernels: 0 us -> 50.1 us
  starting transfers between devices: 37.2 us -> 0 us
  between operations: 15 us -> 0.02 us
  matrix products: 5.1 us -> 0 us
  other arithmetic: 2.84 us -> 0 us
    unnamed x18 -> x11, local copies, waits for them, and re-layouts: 75.9 us -> 3.28 us
    pallas_call x0 -> x1, Pallas kernels: none -> 50.1 us  [on_device(): pl.pallas_call(functools.partial(kernel, clips, sps), out_shape=jax.Shape...]
    all_gather x2 -> x0, waiting for transfers between devices: 37.1 us -> none  [fetch(): gathered = lax.all_gather(local_context[None], 'clip', axis=0, tiled=True)]
    all_to_all x4 -> x0, starting transfers between devices: 31.5 us -> none  [the longest x2 19.3 us: regroup(): lax.all_to_all(features[step_index], 'sp', split_axis=4, concat_axis=3, t...]
    all_to_all x5 -> x0, local copies, waits for them, and re-layouts: 21.2 us -> none  [the longest x3 21.1 us: regroup(): lax.all_to_all(features[step_index], 'sp', split_axis=4, concat_axis=3, t...]
    all_to_all x4 -> x0, waiting for transfers between devices: 17.1 us -> none  [the longest x2 17.1 us: attend_step(): lax.all_to_all(shortened(attended), 'sp', split_axis=2, concat_axis=3, ti...]
    ppermute x2 -> x0, starting transfers between devices: 5.53 us -> none  [the longest x1 3.61 us: padded_2(): lax.ppermute(tail, axis, [(i, (i + 1) % count) for i in range(ends)])]
    dot_general x8 -> x0, matrix products: 5.1 us -> none  [the longest x4 2.59 us: attend_block(): jnp.einsum('qe,ke->qk', query_head, key_heads[head_pos], preferred_elemen...]
  transfers between devices with their start and end apart: 8 -> 0, of which waited for: 4 -> 0; matrix products, arithmetic and copies ran while one was open for 46% -> 0% of each run, Pallas kernels for 0% -> 0%
where the time goes in v1:
time: 53.6 us; the launch traced here: 53.4 us
  Pallas kernels  50.1 us (93%)
  local copies, waits for them, and re-layouts  3.28 us (6%)
    pallas_call x1, Pallas kernels, on_device(): pl.pallas_call(functools.partial(kernel, clips, sps), out_shape=jax.Shape...  50.1 us
    unnamed x11, local copies, waits for them, and re-layouts  3.28 us

profile of v1, /device:TPU:1, one launch (start us, length us, event | category | flops | bytes accessed | tf_op | source)
XLA Modules:
  0.0 53.4 jit_solution(16979613094112295805)
XLA Ops:
  0.0 0.0 copy-start.2
  0.0 0.0 copy-start.3
  0.0 0.0 copy-start.4
  0.0 0.6 %copy-done.2 = s32[32]{0:T(128)S(1)} copy-done((s32[32]{0:T(128)S(1)}, s32[32]{0:T(128)}, u32[]{:S(2)}) %copy-start.2) | copy-done | bytes 152
  0.7 0.0 copy-done.3
  0.7 0.0 copy-done.4
  0.7 0.0 copy-start
  0.7 1.1 %copy-done = bf16[2,3,1,4,8,2048]{5,4,3,2,1,0:T(8,128)(2,1)S(1)} copy-done((bf16[2,3,1,4,8,2048]{5,4,3,2,1,0:T(8,128)(2,1)S(1)}, bf16[2,3,1,4,8,2048]{5,4,3,2,1,0:T(8,128)(2,1)}, u32[]{:S(2)}) %copy-start) | copy-done | bytes 786456
  1.8 0.0 copy-start.1
  1.8 0.8 %copy-done.1 = bf16[1,2,64,128]{3,2,1,0:T(8,128)(2,1)S(1)} copy-done((bf16[1,2,64,128]{3,2,1,0:T(8,128)(2,1)S(1)}, bf16[1,2,64,128]{3,2,1,0:T(8,128)(2,1)}, u32[]{:S(2)}) %copy-start.1) | copy-done | bytes 32792
  2.6 50.1 %shard_map.55 = bf16[2,4,8,2048]{3,2,1,0:T(8,128)(2,1)S(1)} custom-call(bf16[2,3,4,8,2048]{4,3,2,1,0:T(8,128)(2,1)S(1)} %bitcast.7, bf16[16,8,128]{2,1,0:T(8,128)(2,1)S(1)} %bitcast.8, s32[32]{0:T(128)S(1)} %copy-done.2, s32[4]{0:T(128)S(1)} %copy-done.3, s32[2]{0:T(128)S(1)} %bitcast.9), custom_call_target="tpu_custom_call" | custom-call | tf_op jit(solution)/shard_map/pallas_call | solution.py:325
  52.7 0.7 %copy.8 = bf16[2,1,4,8,2048]{4,3,2,1,0:T(8,128)(2,1)} copy(bf16[2,1,4,8,2048]{4,3,2,1,0:T(8,128)(2,1)S(1)} %bitcast.6) | data formatting | bytes 524288
Async XLA Ops:
  0.0 0.7 %copy-start.2 = (s32[32]{0:T(128)S(1)}, s32[32]{0:T(128)}, u32[]{:S(2)}) copy-start(s32[32]{0:T(128)} %cuts.1) | copy-start | bytes 388
  0.0 0.7 %copy-start.3 = (s32[4]{0:T(128)S(1)}, s32[4]{0:T(128)}, u32[]{:S(2)}) copy-start(s32[4]{0:T(128)} %key_clips.1) | copy-start | bytes 52
  0.0 0.7 %copy-start.4 = (s32[1,2]{1,0:T(1,128)S(1)}, s32[1,2]{1,0:T(1,128)}, u32[]{:S(2)}) copy-start(s32[1,2]{1,0:T(1,128)} %param.9) | copy-start | bytes 28
  0.7 1.1 %copy-start = (bf16[2,3,1,4,8,2048]{5,4,3,2,1,0:T(8,128)(2,1)S(1)}, bf16[2,3,1,4,8,2048]{5,4,3,2,1,0:T(8,128)(2,1)}, u32[]{:S(2)}) copy-start(bf16[2,3,1,4,8,2048]{5,4,3,2,1,0:T(8,128)(2,1)} %param.5) | copy-start | bytes 2359300
  1.8 0.8 %copy-start.1 = (bf16[1,2,64,128]{3,2,1,0:T(8,128)(2,1)S(1)}, bf16[1,2,64,128]{3,2,1,0:T(8,128)(2,1)}, u32[]{:S(2)}) copy-start(bf16[1,2,64,128]{3,2,1,0:T(8,128)(2,1)} %param.6) | copy-start | bytes 98308

commit v2 on v1

v2 whole, which is shorter than its diff:
```python
import functools

import jax
import jax.numpy as jnp
from jax import lax
from jax.experimental import pallas as pl
from jax.experimental.pallas import tpu as pltpu
from jax.sharding import PartitionSpec as P

HEAD_DIM = 64
LANES = 128
QUAD = 4
NKEY = 4
MESH = pl.DeviceIdType.MESH


def wait_bytes(ref, sem):
    pltpu.make_async_copy(ref, ref, sem).wait()


def flat(block):
    wide = block.astype(jnp.float32)
    return wide.reshape(-1, LANES).astype(jnp.bfloat16)


def kernel(
    clips,
    sps,
    feat,
    ctx,
    cuts_hbm,
    key_clips_hbm,
    slots_hbm,
    out,
    recv,
    edge,
    pooled,
    scat_0,
    scat_1,
    full_0,
    full_1,
    keys,
    vals,
    done,
    cuts,
    key_clips,
    slots,
    index_sem,
    above_sem,
    in_send,
    in_recv,
    own_sem,
    edge_send,
    edge_recv,
    ex_send,
    ex_recv,
    out_send,
    out_recv,
):
    c = lax.axis_index("clip")
    s = lax.axis_index("sp")
    zs = clips // QUAD
    z = c // QUAD
    q = c % QUAD
    frames = recv.shape[2]
    tiles = ctx.shape[0]
    part = tiles // zs
    frame_rows = sps * 8
    own_rows = frames * frame_rows
    ctx_rows = tiles * 4
    scat, full = (scat_0, scat_1), (full_0, full_1)

    small = [
        pltpu.make_async_copy(src, dst, index_sem.at[i])
        for i, (src, dst) in enumerate(((cuts_hbm, cuts), (key_clips_hbm, key_clips), (slots_hbm, slots)))
    ]
    for copy in small:
        copy.start()

    barrier = pltpu.get_barrier_semaphore()

    def greet(clip, sp):
        pl.semaphore_signal(barrier, inc=1, device_id=(clip, sp), device_id_type=MESH)

    def greet_sp(k, _):
        greet(c, (s + k) % sps)
        return 0

    def greet_quad(k, _):
        greet(z * QUAD + (q + k) % QUAD, s)
        return 0

    lax.fori_loop(1, sps, greet_sp, 0)
    lax.fori_loop(1, QUAD, greet_quad, 0)
    pl.semaphore_wait(barrier, sps - 1 + QUAD - 1 + jnp.where(z > 0, 1, 0))

    @pl.when(z < zs - 1)
    def _():
        greet(c + QUAD, s)

    def report(k, _):
        pl.semaphore_signal(above_sem, inc=1, device_id=(k * QUAD + q, s), device_id_type=MESH)
        return 0

    lax.fori_loop(0, z, report, 0)

    def remote(src, dst, send, rcv, clip, sp):
        pltpu.make_async_remote_copy(
            src_ref=src,
            dst_ref=dst,
            send_sem=send,
            recv_sem=rcv,
            device_id=(clip, sp),
            device_id_type=MESH,
        ).start()

    mid = frames // 2
    groups = (
        (0, 1, 2, 0, 1),
        (0, 1, 2, 1, frames - 1),
        (0, 0, 1, 0, frames),
        (1, 1, 2, 0, frames),
        (1, 0, 1, 0, mid),
        (1, 0, 1, mid, frames - mid),
    )

    def block(group, sp):
        step, low, size, start, count = group
        return feat.at[step, pl.ds(low, size), pl.ds(start, count), :, pl.ds(sp * LANES, LANES)]

    def place(group, sp):
        step, low, size, start, count = group
        return recv.at[step, pl.ds(low, size), pl.ds(start, count), sp]

    def others(group):
        step, low, size, start, count = group
        return recv.at[step, pl.ds(low, size), pl.ds(start, count), pl.ds(0, sps - 1)]

    def own_copy(g):
        return pltpu.make_async_copy(block(groups[g], s), place(groups[g], s), own_sem.at[g])

    def send_group(g):
        def one(k, _):
            to = (s + k) % sps
            remote(block(groups[g], to), place(groups[g], s), in_send.at[g], in_recv.at[g], c, to)
            return 0

        lax.fori_loop(1, sps, one, 0)
        own_copy(g).start()

    def wait_group(g):
        own_copy(g).wait()
        wait_bytes(others(groups[g]), in_recv.at[g])

    def scatter_own(e, src):
        return pltpu.make_async_copy(
            src.at[pl.ds(z * part, part)], scat[e].at[c], own_sem.at[len(groups) + e]
        )

    def scatter(e, src):
        def one(k, _):
            to = (c + clips - k) % clips
            remote(
                src.at[pl.ds((to // QUAD) * part, part)],
                scat[e].at[c],
                ex_send.at[e, 0],
                ex_recv.at[e, 0],
                to,
                s,
            )
            return 0

        scatter_own(e, src).start()
        lax.fori_loop(1, clips, one, 0)

    def gather(e, src):
        scatter_own(e, src).wait()
        wait_bytes(scat[e].at[pl.ds(0, clips - 1)], ex_recv.at[e, 0])
        for i in range(NKEY):
            full[e][z, i] = scat[e][key_clips[i]]

        def one(k, _):
            remote(
                full[e].at[z],
                full[e].at[z],
                ex_send.at[e, 1],
                ex_recv.at[e, 1],
                ((z + k) % zs) * QUAD + q,
                s,
            )
            return 0

        lax.fori_loop(1, zs, one, 0)

    early = z < 3 * zs // 8
    late_groups = range(3, len(groups))
    for g in range(3):
        send_group(g)

    @pl.when(early)
    def _():
        for g in late_groups:
            send_group(g)

    @pl.when(z < zs - 1)
    def _():
        pl.semaphore_wait(above_sem, zs - 1 - z)

    scatter(0, ctx)

    wait_group(0)
    half = tiles // 2
    row = lax.broadcasted_iota(jnp.int32, (half * 8, frame_rows), 0)
    col = lax.broadcasted_iota(jnp.int32, (half * 8, frame_rows), 1)
    pairs = ((col == 2 * row) | (col == 2 * row + 1)).astype(jnp.bfloat16)
    for j in range(2):
        added = jnp.dot(pairs, flat(recv[0, 1 + j, 0]), preferred_element_type=jnp.float32)
        pooled[pl.ds(j * half, half)] = (added * 2**-0.5).reshape(half, 8, LANES).astype(jnp.bfloat16)
    scatter(1, pooled)

    @pl.when(jnp.logical_not(early))
    def _():
        for g in late_groups:
            send_group(g)

    wait_group(1)

    @pl.when(c < clips - 1)
    def _():
        remote(
            recv.at[0, pl.ds(1, 2), frames - 1], edge.at[0], edge_send.at[0], edge_recv.at[0], c + 1, s
        )

    @pl.when(c > 0)
    def _():
        remote(recv.at[0, pl.ds(1, 2), 0], edge.at[1], edge_send.at[1], edge_recv.at[1], c - 1, s)

    @pl.when(c == 0)
    def _():
        edge[0] = jnp.zeros(edge.shape[1:], edge.dtype)

    @pl.when(c == clips - 1)
    def _():
        edge[1] = jnp.zeros(edge.shape[1:], edge.dtype)

    lane = lax.broadcasted_iota(jnp.int32, (1, LANES), 1)
    first = lane < HEAD_DIM

    def put(step, base, key_rows, value_rows, ok=None):
        rows = key_rows.shape[0]
        where = pl.ds(base, rows)
        ones = jnp.ones((rows, LANES), jnp.float32)
        value_rows = value_rows.astype(jnp.float32)
        if ok is not None:
            value_rows = jnp.where(ok, value_rows, 0.0)
            ones = jnp.where(ok, ones, 0.0)
        keys[step, where] = key_rows
        vals[step, 0, where] = jnp.where(first, value_rows, ones).astype(jnp.bfloat16)
        vals[step, 1, where] = jnp.where(first, ones, value_rows).astype(jnp.bfloat16)

    def put_own(step):
        for f in range(frames):
            put(step, f * frame_rows, flat(recv[step, 1, f]), flat(recv[step, 2, f]))

    def put_edge(step, before_ok, after_ok):
        for side, ok in ((0, before_ok), (1, after_ok)):
            own = recv[step, 1, 0].astype(jnp.float32)
            key_rows = jnp.where(ok, edge[side, 0].astype(jnp.float32), own)
            key_rows = key_rows.reshape(-1, LANES).astype(jnp.bfloat16)
            put(step, own_rows + side * frame_rows, key_rows, flat(edge[side, 1]), ok)

    def put_context(step):
        wait_bytes(full[step].at[pl.ds(0, zs - 1)], ex_recv.at[step, 1])
        for i in range(2):
            base = own_rows + 2 * frame_rows + i * ctx_rows
            taken = flat(full[step][:, slots[i]])
            put(step, base, taken[:ctx_rows], taken[ctx_rows:])

    def attend(step, f):
        queries = flat(recv[step, 0, f]).astype(jnp.float32) * HEAD_DIM**-0.5
        both = jnp.concatenate(
            [jnp.where(first, queries, 0.0), jnp.where(first, 0.0, queries)], axis=0
        ).astype(jnp.bfloat16)
        scores = lax.dot_general(
            both, keys[step], (((1,), (1,)), ((), ())), preferred_element_type=jnp.float32
        )
        top = jnp.max(scores, axis=1, keepdims=True)
        weights = jnp.exp(scores - top).astype(jnp.bfloat16)
        left = jnp.dot(weights[:frame_rows], vals[step, 0], preferred_element_type=jnp.float32)
        right = jnp.dot(weights[frame_rows:], vals[step, 1], preferred_element_type=jnp.float32)
        numer = jnp.where(first, left, right)
        total = pltpu.roll(jnp.where(first, right, left), HEAD_DIM, 1)
        done[step, f] = (numer / total).reshape(sps, 8, LANES).astype(jnp.bfloat16)

    parts = ((0, 0, frames), (1, 0, mid), (1, mid, frames - mid))

    def result(p, sp):
        step, start, count = parts[p]
        return done.at[step, pl.ds(start, count), sp]

    def landing(p):
        step, start, count = parts[p]
        return out.at[step, pl.ds(start, count), :, pl.ds(s * LANES, LANES)]

    def own_out(p):
        return pltpu.make_async_copy(result(p, s), landing(p), own_sem.at[len(groups) + 2 + p])

    def send_out(p):
        def one(k, _):
            to = (s + k) % sps
            remote(result(p, to), landing(p), out_send.at[p], out_recv.at[p], c, to)
            return 0

        lax.fori_loop(1, sps, one, 0)
        own_out(p).start()

    for copy in small:
        copy.wait()
    gather(0, ctx)
    put_own(0)
    gather(1, pooled)
    after = jnp.minimum(c + 1, clips - 1)
    before_ok = (c > 0) & (cuts[c] == 0)
    after_ok = (c < clips - 1) & (cuts[after] == 0)
    wait_group(2)

    @pl.when(c > 0)
    def _():
        wait_bytes(edge.at[0], edge_recv.at[0])

    @pl.when(c < clips - 1)
    def _():
        wait_bytes(edge.at[1], edge_recv.at[1])

    put_edge(0, before_ok, after_ok)
    put_context(0)
    for f in range(frames):
        attend(0, f)
    send_out(0)

    wait_group(3)
    put_own(1)
    put_edge(1, before_ok, after_ok)
    put_context(1)
    wait_group(4)
    for f in range(mid):
        attend(1, f)
    send_out(1)
    wait_group(5)
    for f in range(mid, frames):
        attend(1, f)
    send_out(2)

    for g in range(len(groups)):
        wait_bytes(others(groups[g]), in_send.at[g])

    @pl.when(c < clips - 1)
    def _():
        wait_bytes(edge.at[0], edge_send.at[0])

    @pl.when(c > 0)
    def _():
        wait_bytes(edge.at[1], edge_send.at[1])

    for e in range(2):
        wait_bytes(scat[e].at[pl.ds(0, clips - 1)], ex_send.at[e, 0])
        wait_bytes(full[e].at[pl.ds(0, zs - 1)], ex_send.at[e, 1])
    for p in range(len(parts)):
        step, start, count = parts[p]
        all_but_one = done.at[step, pl.ds(start, count), pl.ds(0, sps - 1)]
        wait_bytes(all_but_one, out_send.at[p])
        wait_bytes(all_but_one, out_recv.at[p])
        own_out(p).wait()


def on_device(clips, sps, features, context, scene_cuts, key_clips, owner_slot):
    steps, kinds, _, frames, tokens, width = features.shape
    tiles = context.shape[1] * context.shape[2] // 8
    zs = clips // QUAD
    part = tiles // zs
    key_rows = frames * sps * 8 + 2 * sps * 8 + tiles * 8
    dma = pltpu.SemaphoreType.DMA
    half = jnp.bfloat16
    anywhere = pl.BlockSpec(memory_space=pltpu.HBM)
    mixed = pl.pallas_call(
        functools.partial(kernel, clips, sps),
        out_shape=jax.ShapeDtypeStruct((steps, frames, tokens, width), half),
        in_specs=[anywhere] * 5,
        out_specs=anywhere,
        scratch_shapes=[
            pltpu.VMEM((steps, kinds, frames, sps, 8, LANES), half),
            pltpu.VMEM((2, 2, sps, 8, LANES), half),
            pltpu.VMEM((tiles, 8, LANES), half),
            pltpu.VMEM((clips, part, 8, LANES), half),
            pltpu.VMEM((clips, part, 8, LANES), half),
            pltpu.VMEM((zs, NKEY, part, 8, LANES), half),
            pltpu.VMEM((zs, NKEY, part, 8, LANES), half),
            pltpu.VMEM((2, key_rows, LANES), half),
            pltpu.VMEM((2, 2, key_rows, LANES), half),
            pltpu.VMEM((steps, frames, sps, 8, LANES), half),
            pltpu.SMEM(scene_cuts.shape, jnp.int32),
            pltpu.SMEM(key_clips.shape, jnp.int32),
            pltpu.SMEM((owner_slot.size,), jnp.int32),
            dma((3,)),
            pltpu.SemaphoreType.REGULAR,
            dma((6,)),
            dma((6,)),
            dma((11,)),
            dma((2,)),
            dma((2,)),
            dma((2, 2)),
            dma((2, 2)),
            dma((3,)),
            dma((3,)),
        ],
        compiler_params=pltpu.CompilerParams(
            collective_id=0, has_side_effects=True, vmem_limit_bytes=60 * 2**20
        ),
    )(
        features.reshape(steps, kinds, frames, tokens, width),
        context.reshape(tiles, 8, LANES),
        scene_cuts,
        key_clips,
        owner_slot.reshape(-1),
    )
    return mixed.reshape(steps, 1, frames, tokens, width)


def solution(mesh):
    placed = (
        P(None, None, "clip", None, "sp", None),
        P("clip", None, None, "sp"),
        P(),
        P(),
        P("clip", None),
    )
    return jax.shard_map(
        functools.partial(on_device, mesh.shape["clip"], mesh.shape["sp"]),
        mesh=mesh,
        in_specs=placed,
        out_specs=P(None, "clip", None, "sp", None),
        check_vma=False,
    )
```

time: 53.6 us -> 47.9 us (0.89)
  Pallas kernels: 50.1 us -> 46.1 us
  local copies, waits for them, and re-layouts: 3.28 us -> 1.67 us
    pallas_call x1, Pallas kernels: 50.1 us -> 46.1 us  [on_device(): pl.pallas_call(functools.partial(kernel, clips, sps), out_shape=jax.Shape...]
    unnamed x11 -> x1, local copies, waits for them, and re-layouts: 3.28 us -> 1.67 us
where the time goes in v2:
time: 47.9 us; the launch traced here: 47.8 us
  Pallas kernels  46.1 us (96%)
  local copies, waits for them, and re-layouts  1.67 us (3%)
    pallas_call x1, Pallas kernels, on_device(): pl.pallas_call(functools.partial(kernel, clips, sps), out_shape=jax.Shape...  46.1 us
    unnamed x1, local copies, waits for them, and re-layouts  1.67 us

profile of v2, /device:TPU:1, one launch (start us, length us, event | category | flops | bytes accessed | tf_op | source)
XLA Modules:
  0.0 47.8 jit_solution(13192452332964014599)
XLA Ops:
  0.0 46.1 %shard_map.55 = bf16[2,4,8,2048]{3,2,1,0:T(8,128)(2,1)} custom-call(bf16[2,3,4,8,2048]{4,3,2,1,0:T(8,128)(2,1)} %bitcast.7, bf16[16,8,128]{2,1,0:T(8,128)(2,1)} %bitcast.8, s32[32]{0:T(128)} %cuts_hbm.1, s32[4]{0:T(128)} %key_clips_hbm.1, s32[2]{0:T(128)} %bitcast.9), custom_call_target="tpu_custom_call" | custom-call | tf_op jit(solution)/shard_map/pallas_call | solution.py:385
  46.1 1.7 %copy.8 = bf16[2,1,4,8,2048]{4,3,2,1,0:T(8,128)(2,1)} copy(bf16[2,1,4,8,2048]{4,3,2,1,0:T(8,128)(2,1)} %bitcast.6) | data formatting | bytes 524288

commit v3 on v2

--- a/solution.py
+++ b/solution.py
@@ -41,6 +41,10 @@
     full_1,
     keys,
     vals,
+    queries,
+    tops,
+    numers,
+    totals,
     done,
     cuts,
     key_clips,
@@ -77,32 +81,36 @@
     for copy in small:
         copy.start()
 
+    ring = sps // 2
+
+    def partner(j, across):
+        hops = ring // 2 - (j + 1) // 2
+        y = (s // 2 + jnp.where(j % 2 == 1, hops, ring - hops)) % ring
+        return y * 2 + (s + across) % 2
+
     barrier = pltpu.get_barrier_semaphore()
 
     def greet(clip, sp):
         pl.semaphore_signal(barrier, inc=1, device_id=(clip, sp), device_id_type=MESH)
 
-    def greet_sp(k, _):
-        greet(c, (s + k) % sps)
+    def greet_clip(clip, _):
+        greet(clip, s)
         return 0
 
     def greet_quad(k, _):
         greet(z * QUAD + (q + k) % QUAD, s)
         return 0
 
-    lax.fori_loop(1, sps, greet_sp, 0)
+    for across in (1, 0):
+
+        def greet_sp(j, _):
+            greet(c, partner(j, across))
+            return 0
+
+        lax.fori_loop(0, ring - 1 + across, greet_sp, 0)
     lax.fori_loop(1, QUAD, greet_quad, 0)
-    pl.semaphore_wait(barrier, sps - 1 + QUAD - 1 + jnp.where(z > 0, 1, 0))
-
-    @pl.when(z < zs - 1)
-    def _():
-        greet(c + QUAD, s)
-
-    def report(k, _):
-        pl.semaphore_signal(above_sem, inc=1, device_id=(k * QUAD + q, s), device_id_type=MESH)
-        return 0
-
-    lax.fori_loop(0, z, report, 0)
+    lax.fori_loop((z + 1) * QUAD, clips, greet_clip, 0)
+    pl.semaphore_wait(barrier, sps - 1 + QUAD - 1 + z * QUAD)
 
     def remote(src, dst, send, rcv, clip, sp):
         pltpu.make_async_remote_copy(
@@ -114,14 +122,12 @@
             device_id_type=MESH,
         ).start()
 
-    mid = frames // 2
     groups = (
         (0, 1, 2, 0, 1),
         (0, 1, 2, 1, frames - 1),
         (0, 0, 1, 0, frames),
         (1, 1, 2, 0, frames),
-        (1, 0, 1, 0, mid),
-        (1, 0, 1, mid, frames - mid),
+        (1, 0, 1, 0, frames),
     )
 
     def block(group, sp):
@@ -139,14 +145,13 @@
     def own_copy(g):
         return pltpu.make_async_copy(block(groups[g], s), place(groups[g], s), own_sem.at[g])
 
-    def send_group(g):
-        def one(k, _):
-            to = (s + k) % sps
+    def send_group(g, across):
+        def one(j, _):
+            to = partner(j, across)
             remote(block(groups[g], to), place(groups[g], s), in_send.at[g], in_recv.at[g], c, to)
             return 0
 
-        lax.fori_loop(1, sps, one, 0)
-        own_copy(g).start()
+        lax.fori_loop(0, ring - 1 + across, one, 0)
 
     def wait_group(g):
         own_copy(g).wait()
@@ -158,20 +163,33 @@
         )
 
     def scatter(e, src):
-        def one(k, _):
-            to = (c + clips - k) % clips
+        def one(j, _):
+            hops = zs // 2 - (j // QUAD + 1) // 2
+            plane = (z + jnp.where(j // QUAD % 2 == 1, hops, zs - hops)) % zs
             remote(
-                src.at[pl.ds((to // QUAD) * part, part)],
+                src.at[pl.ds(plane * part, part)],
                 scat[e].at[c],
                 ex_send.at[e, 0],
                 ex_recv.at[e, 0],
-                to,
+                plane * QUAD + (q + 2 + j % QUAD) % QUAD,
                 s,
             )
             return 0
 
+        def near(j, _):
+            remote(
+                src.at[pl.ds(z * part, part)],
+                scat[e].at[c],
+                ex_send.at[e, 0],
+                ex_recv.at[e, 0],
+                z * QUAD + (q + j) % QUAD,
+                s,
+            )
+            return 0
+
         scatter_own(e, src).start()
-        lax.fori_loop(1, clips, one, 0)
+        lax.fori_loop(0, clips - QUAD, one, 0)
+        lax.fori_loop(1, QUAD, near, 0)
 
     def gather(e, src):
         scatter_own(e, src).wait()
@@ -180,34 +198,56 @@
             full[e][z, i] = scat[e][key_clips[i]]
 
         def one(k, _):
-            remote(
-                full[e].at[z],
-                full[e].at[z],
-                ex_send.at[e, 1],
-                ex_recv.at[e, 1],
-                ((z + k) % zs) * QUAD + q,
-                s,
-            )
+            @pl.when(k != z)
+            def _():
+                remote(
+                    full[e].at[z],
+                    full[e].at[z],
+                    ex_send.at[e, 1],
+                    ex_recv.at[e, 1],
+                    k * QUAD + q,
+                    s,
+                )
+
             return 0
 
-        lax.fori_loop(1, zs, one, 0)
-
-    early = z < 3 * zs // 8
-    late_groups = range(3, len(groups))
-    for g in range(3):
-        send_group(g)
+        lax.fori_loop(0, zs, one, 0)
+
+    for across in (1, 0):
+        send_group(0, across)
+    for g in range(len(groups)):
+        own_copy(g).start()
+
+    def report(clip, _):
+        pl.semaphore_signal(above_sem, inc=1, device_id=(clip, s), device_id_type=MESH)
+        return 0
+
+    lax.fori_loop(0, z * QUAD, report, 0)
+
+    @pl.when(z == zs - 1)
+    def _():
+        scatter(0, ctx)
+
+    early = z < zs // 2
 
     @pl.when(early)
     def _():
-        for g in late_groups:
-            send_group(g)
+        for g in (1, 2):
+            send_group(g, 1)
+            send_group(g, 0)
+
+    @pl.when(jnp.logical_not(early))
+    def _():
+        for g in (1, 2):
+            send_group(g, 0)
+
+    for g in (3, 4):
+        send_group(g, 0)
 
     @pl.when(z < zs - 1)
     def _():
-        pl.semaphore_wait(above_sem, zs - 1 - z)
-
-    scatter(0, ctx)
-
+        pl.semaphore_wait(above_sem, (zs - 1 - z) * QUAD)
+        scatter(0, ctx)
     wait_group(0)
     half = tiles // 2
     row = lax.broadcasted_iota(jnp.int32, (half * 8, frame_rows), 0)
@@ -220,8 +260,11 @@
 
     @pl.when(jnp.logical_not(early))
     def _():
-        for g in late_groups:
-            send_group(g)
+        for g in (1, 2):
+            send_group(g, 1)
+
+    for g in (3, 4):
+        send_group(g, 1)
 
     wait_group(1)
 
@@ -276,23 +319,45 @@
             taken = flat(full[step][:, slots[i]])
             put(step, base, taken[:ctx_rows], taken[ctx_rows:])
 
-    def attend(step, f):
-        queries = flat(recv[step, 0, f]).astype(jnp.float32) * HEAD_DIM**-0.5
-        both = jnp.concatenate(
-            [jnp.where(first, queries, 0.0), jnp.where(first, 0.0, queries)], axis=0
+    context_start = own_rows + 2 * frame_rows
+
+    def weigh(step, f, low, count, top):
+        scores = lax.dot_general(
+            queries[step, f],
+            keys[step, pl.ds(low, count)],
+            (((1,), (1,)), ((), ())),
+            preferred_element_type=jnp.float32,
+        )
+        high = jnp.max(scores, axis=1, keepdims=True)
+        if top is not None:
+            high = jnp.maximum(high, top)
+        weights = jnp.exp(scores - high).astype(jnp.bfloat16)
+        where = pl.ds(low, count)
+        left = jnp.dot(weights[:frame_rows], vals[step, 0, where], preferred_element_type=jnp.float32)
+        right = jnp.dot(weights[frame_rows:], vals[step, 1, where], preferred_element_type=jnp.float32)
+        return high, jnp.where(first, left, right), jnp.where(first, right, left)
+
+    def attend_near(step, f):
+        rows = flat(recv[step, 0, f]).astype(jnp.float32) * HEAD_DIM**-0.5
+        queries[step, f] = jnp.concatenate(
+            [jnp.where(first, rows, 0.0), jnp.where(first, 0.0, rows)], axis=0
         ).astype(jnp.bfloat16)
-        scores = lax.dot_general(
-            both, keys[step], (((1,), (1,)), ((), ())), preferred_element_type=jnp.float32
-        )
-        top = jnp.max(scores, axis=1, keepdims=True)
-        weights = jnp.exp(scores - top).astype(jnp.bfloat16)
-        left = jnp.dot(weights[:frame_rows], vals[step, 0], preferred_element_type=jnp.float32)
-        right = jnp.dot(weights[frame_rows:], vals[step, 1], preferred_element_type=jnp.float32)
-        numer = jnp.where(first, left, right)
-        total = pltpu.roll(jnp.where(first, right, left), HEAD_DIM, 1)
+        high, numer, total = weigh(step, f, 0, context_start, None)
+        tops[step, f] = jnp.broadcast_to(high, (2 * frame_rows, LANES))
+        numers[step, f] = numer
+        totals[step, f] = total
+
+    def attend_context(step, f):
+        top = tops[step, f]
+        high, numer, total = weigh(step, f, context_start, 2 * ctx_rows, top[:, :1])
+        scale = jnp.exp(top - high)
+        left, right = scale[:frame_rows], scale[frame_rows:]
+        numer = numer + numers[step, f] * jnp.where(first, left, right)
+        total = total + totals[step, f] * jnp.where(first, right, left)
+        total = pltpu.roll(total, HEAD_DIM, 1)
         done[step, f] = (numer / total).reshape(sps, 8, LANES).astype(jnp.bfloat16)
 
-    parts = ((0, 0, frames), (1, 0, mid), (1, mid, frames - mid))
+    parts = ((0, 0, frames), (1, 0, frames))
 
     def result(p, sp):
         step, start, count = parts[p]
@@ -306,23 +371,23 @@
         return pltpu.make_async_copy(result(p, s), landing(p), own_sem.at[len(groups) + 2 + p])
 
     def send_out(p):
-        def one(k, _):
-            to = (s + k) % sps
-            remote(result(p, to), landing(p), out_send.at[p], out_recv.at[p], c, to)
-            return 0
-
-        lax.fori_loop(1, sps, one, 0)
+        for across in (1, 0):
+
+            def one(j, _):
+                to = partner(j, across)
+                remote(result(p, to), landing(p), out_send.at[p], out_recv.at[p], c, to)
+                return 0
+
+            lax.fori_loop(0, ring - 1 + across, one, 0)
         own_out(p).start()
 
     for copy in small:
         copy.wait()
     gather(0, ctx)
-    put_own(0)
     gather(1, pooled)
     after = jnp.minimum(c + 1, clips - 1)
     before_ok = (c > 0) & (cuts[c] == 0)
     after_ok = (c < clips - 1) & (cuts[after] == 0)
-    wait_group(2)
 
     @pl.when(c > 0)
     def _():
@@ -332,24 +397,19 @@
     def _():
         wait_bytes(edge.at[1], edge_recv.at[1])
 
-    put_edge(0, before_ok, after_ok)
-    put_context(0)
-    for f in range(frames):
-        attend(0, f)
-    send_out(0)
-
-    wait_group(3)
-    put_own(1)
-    put_edge(1, before_ok, after_ok)
-    put_context(1)
-    wait_group(4)
-    for f in range(mid):
-        attend(1, f)
-    send_out(1)
-    wait_group(5)
-    for f in range(mid, frames):
-        attend(1, f)
-    send_out(2)
+    for step in range(2):
+        for g in range(1 + 2 * step, 3 + 2 * step):
+            if g != 1:
+                wait_group(g)
+        put_own(step)
+        put_edge(step, before_ok, after_ok)
+        for f in range(frames):
+            attend_near(step, f)
+    for step in range(2):
+        put_context(step)
+        for f in range(frames):
+            attend_context(step, f)
+        send_out(step)
 
     for g in range(len(groups)):
         wait_bytes(others(groups[g]), in_send.at[g])
@@ -378,15 +438,16 @@
     tiles = context.shape[1] * context.shape[2] // 8
     zs = clips // QUAD
     part = tiles // zs
-    key_rows = frames * sps * 8 + 2 * sps * 8 + tiles * 8
+    frame_rows = sps * 8
+    key_rows = (frames + 2) * frame_rows + tiles * 8
     dma = pltpu.SemaphoreType.DMA
     half = jnp.bfloat16
     anywhere = pl.BlockSpec(memory_space=pltpu.HBM)
     mixed = pl.pallas_call(
         functools.partial(kernel, clips, sps),
-        out_shape=jax.ShapeDtypeStruct((steps, frames, tokens, width), half),
+        out_shape=pltpu.VMEM((steps, frames, tokens, width), half),
         in_specs=[anywhere] * 5,
-        out_specs=anywhere,
+        out_specs=pl.BlockSpec(memory_space=pltpu.VMEM),
         scratch_shapes=[
             pltpu.VMEM((steps, kinds, frames, sps, 8, LANES), half),
             pltpu.VMEM((2, 2, sps, 8, LANES), half),
@@ -397,21 +458,25 @@
             pltpu.VMEM((zs, NKEY, part, 8, LANES), half),
             pltpu.VMEM((2, key_rows, LANES), half),
             pltpu.VMEM((2, 2, key_rows, LANES), half),
+            pltpu.VMEM((steps, frames, 2 * frame_rows, LANES), half),
+            pltpu.VMEM((steps, frames, 2 * frame_rows, LANES), jnp.float32),
+            pltpu.VMEM((steps, frames, frame_rows, LANES), jnp.float32),
+            pltpu.VMEM((steps, frames, frame_rows, LANES), jnp.float32),
             pltpu.VMEM((steps, frames, sps, 8, LANES), half),
             pltpu.SMEM(scene_cuts.shape, jnp.int32),
             pltpu.SMEM(key_clips.shape, jnp.int32),
             pltpu.SMEM((owner_slot.size,), jnp.int32),
             dma((3,)),
             pltpu.SemaphoreType.REGULAR,
-            dma((6,)),
-            dma((6,)),
-            dma((11,)),
+            dma((5,)),
+            dma((5,)),
+            dma((9,)),
             dma((2,)),
             dma((2,)),
             dma((2, 2)),
             dma((2, 2)),
-            dma((3,)),
-            dma((3,)),
+            dma((2,)),
+            dma((2,)),
         ],
         compiler_params=pltpu.CompilerParams(
             collective_id=0, has_side_effects=True, vmem_limit_bytes=60 * 2**20

time: 47.9 us -> 45.6 us (0.952)
  the two profiles are of different devices: /device:TPU:1 before, /device:TPU:64 now
where the time goes in v3:
time: 45.6 us; the launch traced here: 45.5 us
  Pallas kernels  44.7 us (98%)
  local copies, waits for them, and re-layouts  0.71 us (2%)
    pallas_call x1, Pallas kernels, on_device(): pl.pallas_call(functools.partial(kernel, clips, sps), out_shape=pltpu.VME...  44.7 us

profile of v3, /device:TPU:64, one launch (start us, length us, event | category | flops | bytes accessed | tf_op | source)
XLA Modules:
  0.0 45.5 jit_solution(16888403513034631244)
XLA Ops:
  0.0 44.7 %shard_map.55 = bf16[2,4,8,2048]{3,2,1,0:T(8,128)(2,1)S(1)} custom-call(bf16[2,3,4,8,2048]{4,3,2,1,0:T(8,128)(2,1)} %bitcast.7, bf16[16,8,128]{2,1,0:T(8,128)(2,1)} %bitcast.8, s32[32]{0:T(128)} %cuts_hbm.1, s32[4]{0:T(128)} %key_clips_hbm.1, s32[2]{0:T(128)} %bitcast.9), custom_call_target="tpu_custom_call" | custom-call | tf_op jit(solution)/shard_map/pallas_call | solution.py:446
  44.7 0.7 %copy.8 = bf16[2,1,4,8,2048]{4,3,2,1,0:T(8,128)(2,1)} copy(bf16[2,1,4,8,2048]{4,3,2,1,0:T(8,128)(2,1)S(1)} %bitcast.6) | data formatting | bytes 524288

commit v4 on v3

--- a/solution.py
+++ b/solution.py
@@ -229,20 +229,26 @@
         scatter(0, ctx)
 
     early = z < zs // 2
-
-    @pl.when(early)
+    hold = z >= 3 * zs // 4
+
+    @pl.when(jnp.logical_not(hold))
     def _():
         for g in (1, 2):
             send_group(g, 1)
             send_group(g, 0)
 
-    @pl.when(jnp.logical_not(early))
+    @pl.when(hold)
     def _():
         for g in (1, 2):
             send_group(g, 0)
 
     for g in (3, 4):
         send_group(g, 0)
+
+    @pl.when(z < 2)
+    def _():
+        for g in (3, 4):
+            send_group(g, 1)
 
     @pl.when(z < zs - 1)
     def _():
@@ -258,33 +264,15 @@
         pooled[pl.ds(j * half, half)] = (added * 2**-0.5).reshape(half, 8, LANES).astype(jnp.bfloat16)
     scatter(1, pooled)
 
-    @pl.when(jnp.logical_not(early))
+    @pl.when(hold)
     def _():
         for g in (1, 2):
             send_group(g, 1)
 
-    for g in (3, 4):
-        send_group(g, 1)
-
-    wait_group(1)
-
-    @pl.when(c < clips - 1)
-    def _():
-        remote(
-            recv.at[0, pl.ds(1, 2), frames - 1], edge.at[0], edge_send.at[0], edge_recv.at[0], c + 1, s
-        )
-
-    @pl.when(c > 0)
-    def _():
-        remote(recv.at[0, pl.ds(1, 2), 0], edge.at[1], edge_send.at[1], edge_recv.at[1], c - 1, s)
-
-    @pl.when(c == 0)
-    def _():
-        edge[0] = jnp.zeros(edge.shape[1:], edge.dtype)
-
-    @pl.when(c == clips - 1)
-    def _():
-        edge[1] = jnp.zeros(edge.shape[1:], edge.dtype)
+    @pl.when(z >= 2)
+    def _():
+        for g in (3, 4):
+            send_group(g, 1)
 
     lane = lax.broadcasted_iota(jnp.int32, (1, LANES), 1)
     first = lane < HEAD_DIM
@@ -381,35 +369,91 @@
             lax.fori_loop(0, ring - 1 + across, one, 0)
         own_out(p).start()
 
+    def send_edges():
+        wait_group(1)
+
+        @pl.when(c < clips - 1)
+        def _():
+            remote(
+                recv.at[0, pl.ds(1, 2), frames - 1], edge.at[0], edge_send.at[0], edge_recv.at[0], c + 1, s
+            )
+
+        @pl.when(c > 0)
+        def _():
+            remote(recv.at[0, pl.ds(1, 2), 0], edge.at[1], edge_send.at[1], edge_recv.at[1], c - 1, s)
+
+        @pl.when(c == 0)
+        def _():
+            edge[0] = jnp.zeros(edge.shape[1:], edge.dtype)
+
+        @pl.when(c == clips - 1)
+        def _():
+            edge[1] = jnp.zeros(edge.shape[1:], edge.dtype)
+
+    def collect():
+        gather(0, ctx)
+        gather(1, pooled)
+
     for copy in small:
         copy.wait()
-    gather(0, ctx)
-    gather(1, pooled)
+
     after = jnp.minimum(c + 1, clips - 1)
     before_ok = (c > 0) & (cuts[c] == 0)
     after_ok = (c < clips - 1) & (cuts[after] == 0)
 
-    @pl.when(c > 0)
-    def _():
-        wait_bytes(edge.at[0], edge_recv.at[0])
-
-    @pl.when(c < clips - 1)
-    def _():
-        wait_bytes(edge.at[1], edge_recv.at[1])
-
-    for step in range(2):
-        for g in range(1 + 2 * step, 3 + 2 * step):
-            if g != 1:
-                wait_group(g)
+    def near(step):
+        if step == 1:
+            wait_group(3)
         put_own(step)
         put_edge(step, before_ok, after_ok)
+        wait_group(2 + 2 * step)
         for f in range(frames):
             attend_near(step, f)
-    for step in range(2):
+
+    def finish(step):
         put_context(step)
         for f in range(frames):
             attend_context(step, f)
         send_out(step)
+
+    def wait_edges():
+        @pl.when(c > 0)
+        def _():
+            wait_bytes(edge.at[0], edge_recv.at[0])
+
+        @pl.when(c < clips - 1)
+        def _():
+            wait_bytes(edge.at[1], edge_recv.at[1])
+
+    first_planes = z < zs // 4
+
+    @pl.when(first_planes)
+    def _():
+        send_edges()
+        wait_edges()
+        near(0)
+        collect()
+
+    @pl.when(jnp.logical_not(first_planes | hold))
+    def _():
+        send_edges()
+
+    @pl.when(jnp.logical_not(first_planes))
+    def _():
+        collect()
+
+    @pl.when(hold)
+    def _():
+        send_edges()
+
+    @pl.when(jnp.logical_not(first_planes))
+    def _():
+        wait_edges()
+        near(0)
+
+    finish(0)
+    near(1)
+    finish(1)
 
     for g in range(len(groups)):
         wait_bytes(others(groups[g]), in_send.at[g])

time: 45.6 us -> 43.4 us (0.952)
  the two profiles are of different devices: /device:TPU:64 before, /device:TPU:1 now
where the time goes in v4:
time: 43.4 us; the launch traced here: 43.3 us
  Pallas kernels  42.6 us (98%)
  local copies, waits for them, and re-layouts  0.71 us (2%)
    pallas_call x1, Pallas kernels, on_device(): pl.pallas_call(functools.partial(kernel, clips, sps), out_shape=pltpu.VME...  42.6 us

profile of v4, /device:TPU:1, one launch (start us, length us, event | category | flops | bytes accessed | tf_op | source)
XLA Modules:
  0.0 43.3 jit_solution(7081875787876030646)
XLA Ops:
  0.0 42.6 %shard_map.55 = bf16[2,4,8,2048]{3,2,1,0:T(8,128)(2,1)S(1)} custom-call(bf16[2,3,4,8,2048]{4,3,2,1,0:T(8,128)(2,1)} %bitcast.7, bf16[16,8,128]{2,1,0:T(8,128)(2,1)} %bitcast.8, s32[32]{0:T(128)} %cuts_hbm.1, s32[4]{0:T(128)} %key_clips_hbm.1, s32[2]{0:T(128)} %bitcast.9), custom_call_target="tpu_custom_call" | custom-call | tf_op jit(solution)/shard_map/pallas_call | solution.py:490
  42.6 0.7 %copy.8 = bf16[2,1,4,8,2048]{4,3,2,1,0:T(8,128)(2,1)} copy(bf16[2,1,4,8,2048]{4,3,2,1,0:T(8,128)(2,1)S(1)} %bitcast.6) | data formatting | bytes 524288

commit v5 on v4

--- a/solution.py
+++ b/solution.py
@@ -78,8 +78,6 @@
         pltpu.make_async_copy(src, dst, index_sem.at[i])
         for i, (src, dst) in enumerate(((cuts_hbm, cuts), (key_clips_hbm, key_clips), (slots_hbm, slots)))
     ]
-    for copy in small:
-        copy.start()
 
     ring = sps // 2
 
@@ -110,6 +108,8 @@
         lax.fori_loop(0, ring - 1 + across, greet_sp, 0)
     lax.fori_loop(1, QUAD, greet_quad, 0)
     lax.fori_loop((z + 1) * QUAD, clips, greet_clip, 0)
+    for copy in small:
+        copy.start()
     pl.semaphore_wait(barrier, sps - 1 + QUAD - 1 + z * QUAD)
 
     def remote(src, dst, send, rcv, clip, sp):
@@ -164,8 +164,7 @@
 
     def scatter(e, src):
         def one(j, _):
-            hops = zs // 2 - (j // QUAD + 1) // 2
-            plane = (z + jnp.where(j // QUAD % 2 == 1, hops, zs - hops)) % zs
+            plane = (z + 1 + j // QUAD) % zs
             remote(
                 src.at[pl.ds(plane * part, part)],
                 scat[e].at[c],
@@ -280,14 +279,13 @@
     def put(step, base, key_rows, value_rows, ok=None):
         rows = key_rows.shape[0]
         where = pl.ds(base, rows)
-        ones = jnp.ones((rows, LANES), jnp.float32)
-        value_rows = value_rows.astype(jnp.float32)
+        ones = jnp.ones((rows, LANES), jnp.bfloat16)
         if ok is not None:
-            value_rows = jnp.where(ok, value_rows, 0.0)
-            ones = jnp.where(ok, ones, 0.0)
+            value_rows = jnp.where(ok, value_rows, jnp.zeros_like(value_rows))
+            ones = jnp.where(ok, ones, jnp.zeros_like(ones))
         keys[step, where] = key_rows
-        vals[step, 0, where] = jnp.where(first, value_rows, ones).astype(jnp.bfloat16)
-        vals[step, 1, where] = jnp.where(first, ones, value_rows).astype(jnp.bfloat16)
+        vals[step, 0, where] = jnp.where(first, value_rows, ones)
+        vals[step, 1, where] = jnp.where(first, ones, value_rows)
 
     def put_own(step):
         for f in range(frames):
@@ -321,17 +319,28 @@
             high = jnp.maximum(high, top)
         weights = jnp.exp(scores - high).astype(jnp.bfloat16)
         where = pl.ds(low, count)
-        left = jnp.dot(weights[:frame_rows], vals[step, 0, where], preferred_element_type=jnp.float32)
-        right = jnp.dot(weights[frame_rows:], vals[step, 1, where], preferred_element_type=jnp.float32)
+        left = jnp.dot(weights[:block_rows], vals[step, 0, where], preferred_element_type=jnp.float32)
+        right = jnp.dot(weights[block_rows:], vals[step, 1, where], preferred_element_type=jnp.float32)
         return high, jnp.where(first, left, right), jnp.where(first, right, left)
 
+    columns = max(ring // 4, 1)
+    blocks = ring // columns
+    part_rows = 2 * frames * 8
+    block_rows = columns * part_rows
+
+    def origins(f):
+        for j in range(f * columns, (f + 1) * columns):
+            hops = ring // 2 - (j + 1) // 2
+            yield hops, (s // 2 + (hops if j % 2 == 1 else ring - hops)) % ring * 2
+
     def attend_near(step, f):
-        rows = flat(recv[step, 0, f]).astype(jnp.float32) * HEAD_DIM**-0.5
+        rows = [flat(recv[step, 0, :, pl.ds(low, 2)]) for _, low in origins(f)]
+        rows = jnp.concatenate(rows, axis=0).astype(jnp.float32) * HEAD_DIM**-0.5
         queries[step, f] = jnp.concatenate(
             [jnp.where(first, rows, 0.0), jnp.where(first, 0.0, rows)], axis=0
         ).astype(jnp.bfloat16)
         high, numer, total = weigh(step, f, 0, context_start, None)
-        tops[step, f] = jnp.broadcast_to(high, (2 * frame_rows, LANES))
+        tops[step, f] = jnp.broadcast_to(high, (2 * block_rows, LANES))
         numers[step, f] = numer
         totals[step, f] = total
 
@@ -339,35 +348,28 @@
         top = tops[step, f]
         high, numer, total = weigh(step, f, context_start, 2 * ctx_rows, top[:, :1])
         scale = jnp.exp(top - high)
-        left, right = scale[:frame_rows], scale[frame_rows:]
+        left, right = scale[:block_rows], scale[block_rows:]
         numer = numer + numers[step, f] * jnp.where(first, left, right)
         total = total + totals[step, f] * jnp.where(first, right, left)
         total = pltpu.roll(total, HEAD_DIM, 1)
-        done[step, f] = (numer / total).reshape(sps, 8, LANES).astype(jnp.bfloat16)
-
-    parts = ((0, 0, frames), (1, 0, frames))
-
-    def result(p, sp):
-        step, start, count = parts[p]
-        return done.at[step, pl.ds(start, count), sp]
-
-    def landing(p):
-        step, start, count = parts[p]
-        return out.at[step, pl.ds(start, count), :, pl.ds(s * LANES, LANES)]
-
-    def own_out(p):
-        return pltpu.make_async_copy(result(p, s), landing(p), own_sem.at[len(groups) + 2 + p])
-
-    def send_out(p):
-        for across in (1, 0):
-
-            def one(j, _):
-                to = partner(j, across)
-                remote(result(p, to), landing(p), out_send.at[p], out_recv.at[p], c, to)
-                return 0
-
-            lax.fori_loop(0, ring - 1 + across, one, 0)
-        own_out(p).start()
+        mixed = numer / total
+        for m, (_, low) in enumerate(origins(f)):
+            rows = mixed[m * part_rows : (m + 1) * part_rows]
+            done[step, :, pl.ds(low, 2)] = rows.reshape(frames, 2, 8, LANES).astype(jnp.bfloat16)
+
+    def landing(step):
+        return out.at[step, :, :, pl.ds(s * LANES, LANES)]
+
+    def own_out(step):
+        return pltpu.make_async_copy(done.at[step, :, s], landing(step), own_sem.at[len(groups) + 2 + step])
+
+    def send_out(step, f):
+        for hops, low in origins(f):
+            for to in (low + (s + 1) % 2, low + s % 2):
+
+                @pl.when(to != s)
+                def _():
+                    remote(done.at[step, :, to], landing(step), out_send.at[step], out_recv.at[step], c, to)
 
     def send_edges():
         wait_group(1)
@@ -401,20 +403,34 @@
     before_ok = (c > 0) & (cuts[c] == 0)
     after_ok = (c < clips - 1) & (cuts[after] == 0)
 
-    def near(step):
+    def put_near(step):
         if step == 1:
             wait_group(3)
         put_own(step)
         put_edge(step, before_ok, after_ok)
+
+    def near(step):
+        put_near(step)
         wait_group(2 + 2 * step)
-        for f in range(frames):
+        for f in range(blocks):
             attend_near(step, f)
 
     def finish(step):
         put_context(step)
-        for f in range(frames):
+        for f in range(blocks):
             attend_context(step, f)
-        send_out(step)
+            send_out(step, f)
+        own_out(step).start()
+
+    def whole(step):
+        put_near(step)
+        put_context(step)
+        wait_group(2 + 2 * step)
+        for f in range(blocks):
+            attend_near(step, f)
+            attend_context(step, f)
+            send_out(step, f)
+        own_out(step).start()
 
     def wait_edges():
         @pl.when(c > 0)
@@ -433,6 +449,7 @@
         wait_edges()
         near(0)
         collect()
+        near(1)
 
     @pl.when(jnp.logical_not(first_planes | hold))
     def _():
@@ -452,8 +469,14 @@
         near(0)
 
     finish(0)
-    near(1)
-    finish(1)
+
+    @pl.when(first_planes)
+    def _():
+        finish(1)
+
+    @pl.when(jnp.logical_not(first_planes))
+    def _():
+        whole(1)
 
     for g in range(len(groups)):
         wait_bytes(others(groups[g]), in_send.at[g])
@@ -469,12 +492,11 @@
     for e in range(2):
         wait_bytes(scat[e].at[pl.ds(0, clips - 1)], ex_send.at[e, 0])
         wait_bytes(full[e].at[pl.ds(0, zs - 1)], ex_send.at[e, 1])
-    for p in range(len(parts)):
-        step, start, count = parts[p]
-        all_but_one = done.at[step, pl.ds(start, count), pl.ds(0, sps - 1)]
-        wait_bytes(all_but_one, out_send.at[p])
-        wait_bytes(all_but_one, out_recv.at[p])
-        own_out(p).wait()
+    for step in range(2):
+        all_but_one = done.at[step, :, pl.ds(0, sps - 1)]
+        wait_bytes(all_but_one, out_send.at[step])
+        wait_bytes(all_but_one, out_recv.at[step])
+        own_out(step).wait()
 
 
 def on_device(clips, sps, features, context, scene_cuts, key_clips, owner_slot):
@@ -483,6 +505,8 @@
     zs = clips // QUAD
     part = tiles // zs
     frame_rows = sps * 8
+    blocks = sps // 2 // max(sps // 8, 1)
+    block_rows = frames * frame_rows // blocks
     key_rows = (frames + 2) * frame_rows + tiles * 8
     dma = pltpu.SemaphoreType.DMA
     half = jnp.bfloat16
@@ -502,10 +526,10 @@
             pltpu.VMEM((zs, NKEY, part, 8, LANES), half),
             pltpu.VMEM((2, key_rows, LANES), half),
             pltpu.VMEM((2, 2, key_rows, LANES), half),
-            pltpu.VMEM((steps, frames, 2 * frame_rows, LANES), half),
-            pltpu.VMEM((steps, frames, 2 * frame_rows, LANES), jnp.float32),
-            pltpu.VMEM((steps, frames, frame_rows, LANES), jnp.float32),
-            pltpu.VMEM((steps, frames, frame_rows, LANES), jnp.float32),
+            pltpu.VMEM((steps, blocks, 2 * block_rows, LANES), half),
+            pltpu.VMEM((steps, blocks, 2 * block_rows, LANES), jnp.float32),
+            pltpu.VMEM((steps, blocks, block_rows, LANES), jnp.float32),
+            pltpu.VMEM((steps, blocks, block_rows, LANES), jnp.float32),
             pltpu.VMEM((steps, frames, sps, 8, LANES), half),
             pltpu.SMEM(scene_cuts.shape, jnp.int32),
             pltpu.SMEM(key_clips.shape, jnp.int32),

time: 43.4 us -> 42.7 us (0.984)
  Pallas kernels: 42.6 us -> 41.9 us
    pallas_call x1, Pallas kernels: 42.6 us -> 41.9 us  [on_device(): pl.pallas_call(functools.partial(kernel, clips, sps), out_shape=pltpu.VME...]
where the time goes in v5:
time: 42.7 us; the launch traced here: 42.6 us
  Pallas kernels  41.9 us (98%)
  local copies, waits for them, and re-layouts  0.71 us (2%)
    pallas_call x1, Pallas kernels, on_device(): pl.pallas_call(functools.partial(kernel, clips, sps), out_shape=pltpu.VME...  41.9 us

profile of v5, /device:TPU:1, one launch (start us, length us, event | category | flops | bytes accessed | tf_op | source)
XLA Modules:
  0.0 42.6 jit_solution(6866250073571525426)
XLA Ops:
  0.0 41.9 %shard_map.55 = bf16[2,4,8,2048]{3,2,1,0:T(8,128)(2,1)S(1)} custom-call(bf16[2,3,4,8,2048]{4,3,2,1,0:T(8,128)(2,1)} %bitcast.7, bf16[16,8,128]{2,1,0:T(8,128)(2,1)} %bitcast.8, s32[32]{0:T(128)} %cuts_hbm.1, s32[4]{0:T(128)} %key_clips_hbm.1, s32[2]{0:T(128)} %bitcast.9), custom_call_target="tpu_custom_call" | custom-call | tf_op jit(solution)/shard_map/pallas_call | solution.py:514
  41.9 0.7 %copy.8 = bf16[2,1,4,8,2048]{4,3,2,1,0:T(8,128)(2,1)} copy(bf16[2,1,4,8,2048]{4,3,2,1,0:T(8,128)(2,1)S(1)} %bitcast.6) | data formatting | bytes 524288

commit v6 on v5

--- a/solution.py
+++ b/solution.py
@@ -187,8 +187,8 @@
             return 0
 
         scatter_own(e, src).start()
-        lax.fori_loop(0, clips - QUAD, one, 0)
-        lax.fori_loop(1, QUAD, near, 0)
+        lax.fori_loop(0, clips - QUAD, one, 0, unroll=QUAD)
+        lax.fori_loop(1, QUAD, near, 0, unroll=True)
 
     def gather(e, src):
         scatter_own(e, src).wait()

time: 42.7 us -> 42.3 us (level)
  Pallas kernels: 41.9 us -> 41.4 us
    pallas_call x1, Pallas kernels: 41.9 us -> 41.4 us  [on_device(): pl.pallas_call(functools.partial(kernel, clips, sps), out_shape=pltpu.VME...]
where the time goes in v6:
time: 42.3 us; the launch traced here: 42.1 us
  Pallas kernels  41.4 us (98%)
  local copies, waits for them, and re-layouts  0.71 us (2%)
    pallas_call x1, Pallas kernels, on_device(): pl.pallas_call(functools.partial(kernel, clips, sps), out_shape=pltpu.VME...  41.4 us

profile of v6, /device:TPU:1, one launch (start us, length us, event | category | flops | bytes accessed | tf_op | source)
XLA Modules:
  0.0 42.1 jit_solution(5414170762046356293)
XLA Ops:
  0.0 41.4 %shard_map.55 = bf16[2,4,8,2048]{3,2,1,0:T(8,128)(2,1)S(1)} custom-call(bf16[2,3,4,8,2048]{4,3,2,1,0:T(8,128)(2,1)} %bitcast.7, bf16[16,8,128]{2,1,0:T(8,128)(2,1)} %bitcast.8, s32[32]{0:T(128)} %cuts_hbm.1, s32[4]{0:T(128)} %key_clips_hbm.1, s32[2]{0:T(128)} %bitcast.9), custom_call_target="tpu_custom_call" | custom-call | tf_op jit(solution)/shard_map/pallas_call | solution.py:514
  41.4 0.7 %copy.8 = bf16[2,1,4,8,2048]{4,3,2,1,0:T(8,128)(2,1)} copy(bf16[2,1,4,8,2048]{4,3,2,1,0:T(8,128)(2,1)S(1)} %bitcast.6) | data formatting | bytes 524288

commit v7 on v6

--- a/solution.py
+++ b/solution.py
@@ -210,7 +210,7 @@
 
             return 0
 
-        lax.fori_loop(0, zs, one, 0)
+        lax.fori_loop(0, zs, one, 0, unroll=True)
 
     for across in (1, 0):
         send_group(0, across)

time: 42.3 us -> 42.3 us (level)
  no operation moved by 1% of the time
where the time goes in v7:
time: 42.3 us; the launch traced here: 42.1 us
  Pallas kernels  41.4 us (98%)
  local copies, waits for them, and re-layouts  0.71 us (2%)
    pallas_call x1, Pallas kernels, on_device(): pl.pallas_call(functools.partial(kernel, clips, sps), out_shape=pltpu.VME...  41.4 us

profile of v7, /device:TPU:1, one launch (start us, length us, event | category | flops | bytes accessed | tf_op | source)
XLA Modules:
  0.0 42.1 jit_solution(10196755460644323250)
XLA Ops:
  0.0 41.4 %shard_map.55 = bf16[2,4,8,2048]{3,2,1,0:T(8,128)(2,1)S(1)} custom-call(bf16[2,3,4,8,2048]{4,3,2,1,0:T(8,128)(2,1)} %bitcast.7, bf16[16,8,128]{2,1,0:T(8,128)(2,1)} %bitcast.8, s32[32]{0:T(128)} %cuts_hbm.1, s32[4]{0:T(128)} %key_clips_hbm.1, s32[2]{0:T(128)} %bitcast.9), custom_call_target="tpu_custom_call" | custom-call | tf_op jit(solution)/shard_map/pallas_call | solution.py:514
  41.4 0.7 %copy.8 = bf16[2,1,4,8,2048]{4,3,2,1,0:T(8,128)(2,1)} copy(bf16[2,1,4,8,2048]{4,3,2,1,0:T(8,128)(2,1)S(1)} %bitcast.6) | data formatting | bytes 524288
